TPU v7x, 32 devices: a whole 2x2x4 slice. The times are simulated.
32 devices in a mesh: dp: 8 (over y, x, core), tensor: 4 (over z).
Axes of the slice: x: 2, y: 2, z: 4, core: 2. Of those that a mesh axis runs over, the one named last changes fastest.
Arguments:
- block_in: bfloat16 [4096, 768], P(('dp', 'tensor')), may hold values from -6 to 6
- segment_ids: int32 [8, 512], P('dp'), may hold values from 0 to 3, never falling along the last dimension, each value on 1 to 384 neighbouring positions
- first_norm_gain: float32 [768], replicated, may hold values from 0.5 to 1.5
- first_norm_bias: float32 [768], replicated, may hold values from -3 to 3
- qkv_weight: bfloat16 [768, 3, 768], P(None, None, 'tensor'), may hold values from -1 to 1
- qv_bias: float32 [2, 768], P(None, 'tensor'), may hold values from -3 to 3
- out_weight: bfloat16 [768, 768], P('tensor'), may hold values from -0.875 to 0.875
- out_bias: float32 [768], replicated, may hold values from -3 to 3
- second_norm_gain: float32 [768], replicated, may hold values from 0.5 to 1.5
- second_norm_bias: float32 [768], replicated, may hold values from -3 to 3
- fc_weight: bfloat16 [768, 3072], P(None, 'tensor'), may hold values from -0.21875 to 0.21875
- fc_bias: float32 [3072], P('tensor'), may hold values from -3 to 3
- proj_weight: bfloat16 [3072, 768], P('tensor'), may hold values from -0.109375 to 0.109375
- proj_bias: float32 [768], replicated, may hold values from -3 to 3
- out_grad: bfloat16 [4096, 768], P(('dp', 'tensor')), may hold values from -6 to 6
Outputs:
- block_out: float32 [4096, 768], P(('dp', 'tensor'))
- d_in: float32 [4096, 768], P(('dp', 'tensor'))
- d_ln1_gain: float32 [768], replicated
- d_ln1_bias: float32 [768], replicated
- d_qkv_weight: float32 [768, 3, 768], P(None, None, 'tensor')
- d_qv_bias: float32 [2, 768], P(None, 'tensor')
- d_out_weight: float32 [768, 768], P('tensor')
- d_out_bias: float32 [768], replicated
- d_ln2_gain: float32 [768], replicated
- d_ln2_bias: float32 [768], replicated
- d_fc_weight: float32 [768, 3072], P(None, 'tensor')
- d_fc_bias: float32 [3072], P('tensor')
- d_proj_weight: float32 [3072, 768], P('tensor')
- d_proj_bias: float32 [768], replicated
Inputs may be any that keep to these rules, and one draw needn't show every extreme that they name: `segment_ids`: within each row of 512 tokens the numbers never fall.
All inputs are finite; a program needn't handle non-finite values.
Results may differ from a plain program's by a relative error of at most 0.012.
Values may be sent and summed in bfloat16 or wider, within the bound.
A program may use at most 64 MiB of HBM per device.

v0:
```python
import math

import jax
import jax.numpy as jnp
from jax import lax
from jax.sharding import PartitionSpec as P

HD = 64


EPS = 1e-05
GELU_C = math.sqrt(2.0 / math.pi)


def apply_layer_norm(values, scale_gain, shift_bias):
    centered_input = values - jnp.mean(values, axis=-1, keepdims=True)
    variance = jnp.mean(centered_input * centered_input, axis=-1, keepdims=True)
    inverse_deviation = lax.rsqrt(variance + EPS)
    normalized_input = centered_input * inverse_deviation
    return (normalized_input * scale_gain + shift_bias, normalized_input, inverse_deviation)


def layer_norm_backward(upstream_gradient, normalized_input, inverse_deviation, scale_gain):
    scaled_gradient = upstream_gradient * scale_gain
    incoming_gradient = inverse_deviation * (
        scaled_gradient
        - jnp.mean(scaled_gradient, axis=-1, keepdims=True)
        - normalized_input * jnp.mean(scaled_gradient * normalized_input, axis=-1, keepdims=True)
    )
    return (
        incoming_gradient,
        jnp.sum(upstream_gradient * normalized_input, axis=0),
        jnp.sum(upstream_gradient, axis=0),
    )


def gelu(value):
    return 0.5 * value * (1.0 + jnp.tanh(GELU_C * (value + 0.044715 * value**3)))


def gelu_grad(value):
    tangent = jnp.tanh(GELU_C * (value + 0.044715 * value**3))
    return 0.5 * (1.0 + tangent) + 0.5 * value * (1.0 - tangent * tangent) * GELU_C * (
        1.0 + 3.0 * 0.044715 * value * value
    )


def gather_rows(values):
    return lax.all_gather(values, "tensor", axis=0, tiled=True)


def scatter_rows(values):
    return lax.psum_scatter(values, "tensor", scatter_dimension=0, tiled=True)


def masked_scores(query, key, segs):
    length = segs.shape[0]
    scores = jnp.einsum("qhd,khd->hqk", query, key, preferred_element_type=jnp.float32) * 0.125
    rows = jnp.arange(length)
    allowed = (segs[:, None] == segs[None, :]) & (rows[:, None] >= rows[None, :])
    return jnp.where(allowed[None], scores, -1e30)


def attend(items):
    query, key, value, segs = items
    scores = masked_scores(query, key, segs)
    top = jnp.max(scores, axis=-1, keepdims=True)
    lse = top[..., 0] + jnp.log(jnp.sum(jnp.exp(scores - top), axis=-1))
    weights = jnp.exp(scores - lse[..., None]).astype(jnp.bfloat16)
    output = jnp.einsum("hqk,khd->qhd", weights, value, preferred_element_type=jnp.float32)
    return (output.astype(jnp.bfloat16), lse)


def attend_back(items):
    query, key, value, segs, output, lse, d_out = items
    weights = jnp.exp(masked_scores(query, key, segs) - lse[..., None])
    rounded = weights.astype(jnp.bfloat16)
    d_value = jnp.einsum("hqk,qhd->khd", rounded, d_out, preferred_element_type=jnp.float32)
    d_probs = jnp.einsum("qhd,khd->hqk", d_out, value, preferred_element_type=jnp.float32)
    delta = jnp.transpose(jnp.sum(d_out.astype(jnp.float32) * output.astype(jnp.float32), axis=-1))
    d_scores = (weights * (d_probs - delta[..., None]) * 0.125).astype(jnp.bfloat16)
    d_query = jnp.einsum("hqk,khd->qhd", d_scores, key, preferred_element_type=jnp.float32)
    d_key = jnp.einsum("hqk,qhd->khd", d_scores, query, preferred_element_type=jnp.float32)
    return (d_query.astype(jnp.bfloat16), d_key.astype(jnp.bfloat16), d_value.astype(jnp.bfloat16))


def on_device(
    block_in,
    segment_ids,
    first_norm_gain,
    first_norm_bias,
    qkv_weight,
    qv_bias,
    out_weight,
    out_bias,
    second_norm_gain,
    second_norm_bias,
    fc_weight,
    fc_bias,
    proj_weight,
    proj_bias,
    out_grad,
):
    width = block_in.shape[1]
    local_width = qkv_weight.shape[2]
    heads_dev = local_width // HD
    seq_count = segment_ids.shape[0]
    length = segment_ids.shape[1]
    factor = 1.0 / (seq_count * lax.axis_size("dp"))
    wqkv = qkv_weight.reshape(width, 3 * local_width)
    bias_row = jnp.concatenate([qv_bias[0], jnp.zeros_like(qv_bias[0]), qv_bias[1]])
    layer_input = block_in.astype(jnp.float32)
    first_norm_output, first_normalized_input, first_inverse_deviation = apply_layer_norm(
        layer_input, first_norm_gain, first_norm_bias
    )
    full1 = gather_rows(first_norm_output.astype(jnp.bfloat16))
    qkv = (jnp.dot(full1, wqkv, preferred_element_type=jnp.float32) + bias_row).astype(jnp.bfloat16)
    parts = qkv.reshape(seq_count, length, 3, heads_dev, HD)
    query, key, value = (parts[:, :, 0], parts[:, :, 1], parts[:, :, 2])
    output, lse = lax.map(attend, (query, key, value, segment_ids))
    flat = output.reshape(seq_count * length, local_width)
    middle_state = (
        layer_input
        + scatter_rows(jnp.dot(flat, out_weight, preferred_element_type=jnp.float32))
        + out_bias
    )
    second_norm_output, second_normalized_input, second_inverse_deviation = apply_layer_norm(
        middle_state, second_norm_gain, second_norm_bias
    )
    full2 = gather_rows(second_norm_output.astype(jnp.bfloat16))
    pre = jnp.dot(full2, fc_weight, preferred_element_type=jnp.float32) + fc_bias
    act = gelu(pre).astype(jnp.bfloat16)
    block_out = (
        middle_state
        + scatter_rows(jnp.dot(act, proj_weight, preferred_element_type=jnp.float32))
        + proj_bias
    )
    grad_full = gather_rows(out_grad)
    g_proj_w = jnp.dot(act.T, grad_full, preferred_element_type=jnp.float32) * factor
    d_pre = (
        jnp.dot(grad_full, proj_weight.T, preferred_element_type=jnp.float32) * gelu_grad(pre)
    ).astype(jnp.bfloat16)
    g_fc_w = jnp.dot(full2.T, d_pre, preferred_element_type=jnp.float32) * factor
    g_fc_b = jnp.sum(d_pre.astype(jnp.float32), axis=0) * factor
    second_norm_gradient = scatter_rows(
        jnp.dot(d_pre, fc_weight.T, preferred_element_type=jnp.float32)
    )
    cotf = out_grad.astype(jnp.float32)
    partial_gradient, second_norm_gain_gradient, second_norm_bias_gradient = layer_norm_backward(
        second_norm_gradient, second_normalized_input, second_inverse_deviation, second_norm_gain
    )
    d_mid = cotf + partial_gradient
    g_proj_b = jnp.sum(cotf, axis=0) * factor
    g_out_b = jnp.sum(d_mid, axis=0) * factor
    mid_full = gather_rows(d_mid.astype(jnp.bfloat16))
    g_out_w = jnp.dot(flat.T, mid_full, preferred_element_type=jnp.float32) * factor
    d_o = jnp.dot(mid_full, out_weight.T, preferred_element_type=jnp.float32).astype(jnp.bfloat16)
    d_o = d_o.reshape(seq_count, length, heads_dev, HD)
    d_query, d_key, d_value = lax.map(
        attend_back, (query, key, value, segment_ids, output, lse, d_o)
    )
    d_qkv = jnp.stack([d_query, d_key, d_value], axis=2).reshape(
        seq_count * length, 3 * local_width
    )
    g_qkv_w = (jnp.dot(full1.T, d_qkv, preferred_element_type=jnp.float32) * factor).reshape(
        width, 3, local_width
    )
    query_sum = jnp.sum(d_query.astype(jnp.float32), axis=(0, 1)).reshape(local_width)
    value_sum = jnp.sum(d_value.astype(jnp.float32), axis=(0, 1)).reshape(local_width)
    g_qv_b = jnp.stack([query_sum, value_sum]) * factor
    first_norm_gradient = scatter_rows(jnp.dot(d_qkv, wqkv.T, preferred_element_type=jnp.float32))
    partial_gradient1, first_norm_gain_gradient, first_norm_bias_gradient = layer_norm_backward(
        first_norm_gradient, first_normalized_input, first_inverse_deviation, first_norm_gain
    )
    d_in = d_mid + partial_gradient1
    first_norm_gain_gradient = first_norm_gain_gradient * factor
    first_norm_bias_gradient = first_norm_bias_gradient * factor
    second_norm_gain_gradient = second_norm_gain_gradient * factor
    second_norm_bias_gradient = second_norm_bias_gradient * factor
    g_qkv_w, g_qv_b, g_out_w, g_proj_w, g_fc_w, g_fc_b = lax.psum(
        (g_qkv_w, g_qv_b, g_out_w, g_proj_w, g_fc_w, g_fc_b), "dp"
    )
    (
        first_norm_gain_gradient,
        first_norm_bias_gradient,
        g_out_b,
        second_norm_gain_gradient,
        second_norm_bias_gradient,
        g_proj_b,
    ) = lax.psum(
        (
            first_norm_gain_gradient,
            first_norm_bias_gradient,
            g_out_b,
            second_norm_gain_gradient,
            second_norm_bias_gradient,
            g_proj_b,
        ),
        ("dp", "tensor"),
    )
    return (
        block_out,
        d_in,
        first_norm_gain_gradient,
        first_norm_bias_gradient,
        g_qkv_w,
        g_qv_b,
        g_out_w,
        g_out_b,
        second_norm_gain_gradient,
        second_norm_bias_gradient,
        g_fc_w,
        g_fc_b,
        g_proj_w,
        g_proj_b,
    )


def solution(mesh):
    return jax.shard_map(
        on_device,
        mesh=mesh,
        in_specs=(
            P(("dp", "tensor"), None),
            P("dp", None),
            P(),
            P(),
            P(None, None, "tensor"),
            P(None, "tensor"),
            P("tensor", None),
            P(),
            P(),
            P(),
            P(None, "tensor"),
            P("tensor"),
            P("tensor", None),
            P(),
            P(("dp", "tensor"), None),
        ),
        out_specs=(
            P(("dp", "tensor"), None),
            P(("dp", "tensor"), None),
            P(),
            P(),
            P(None, None, "tensor"),
            P(None, "tensor"),
            P("tensor", None),
            P(),
            P(),
            P(),
            P(None, "tensor"),
            P("tensor"),
            P("tensor", None),
            P(),
        ),
        check_vma=False,
    )
```

profile of v0, /device:TPU:17, one launch (start us, length us, event | category | flops | bytes accessed | tf_op | source)
XLA Modules:
  0.0 373.5 jit_solution(17702382596368259676)
XLA Ops:
  7.3 1.2 convert_reduce_fusion.1
  8.5 1.1 fusion.27
  10.7 15.7 %all_gather.12 = bf16[512,768]{1,0:T(8,128)(2,1)S(1)} all-gather(bf16[128,768]{1,0:T(8,128)(2,1)S(1)} %fusion.21), channel_id=1, replica_groups=mesh['dp'=8,'tensor'=4] {'tensor'}, dimensions={0}, use_global_device_ids=true | all-gather | bytes 983040 | tf_op jit(solution)/shard_map/all_gather | solution.py:49
  31.0 1.6 fusion.37
  32.6 23.5 %all_gather.14 = bf16[512,768]{1,0:T(8,128)(2,1)} all-gather(bf16[128,768]{1,0:T(8,128)(2,1)S(1)} %copy-done.19), channel_id=1, replica_groups=mesh['dp'=8,'tensor'=4] {'tensor'}, dimensions={0}, use_global_device_ids=true | all-gather | bytes 983040 | tf_op jit(solution)/shard_map/all_gather | solution.py:49
  56.1 22.1 %reduce-scatter.5.cloned.1.call-done = f32[128,768]{1,0:T(8,128)} async-done(((f32[512,768]{1,0:T(8,128)}), f32[128,768]{1,0:T(8,128)}) %reduce-scatter.5.cloned.1.call-update) | async-done | bytes 393232 | tf_op jit(solution)/shard_map/reduce_scatter | solution.py:53
  78.2 1.2 fusion.34
  79.8 15.4 %all_gather.13 = bf16[512,768]{1,0:T(8,128)(2,1)S(1)} all-gather(bf16[128,768]{1,0:T(8,128)(2,1)S(1)} %add_convert_fusion), channel_id=1, replica_groups=mesh['dp'=8,'tensor'=4] {'tensor'}, dimensions={0}, use_global_device_ids=true | all-gather | bytes 983040 | tf_op jit(solution)/shard_map/all_gather | solution.py:49
  96.4 2.9 convert_reduce_fusion
  99.3 3.1 fusion.38
  102.5 3.6 fusion.32
  106.1 33.9 %reduce-scatter.9.cloned.1.call-done = f32[128,768]{1,0:T(8,128)} async-done(((f32[512,768]{1,0:T(8,128)}), f32[128,768]{1,0:T(8,128)}) %reduce-scatter.9.cloned.1.call-update) | async-done | bytes 393232 | tf_op jit(solution)/shard_map/reduce_scatter | solution.py:53
  140.1 1.2 multiply_reduce_fusion
  141.3 35.9 %reduce-scatter.7.cloned.1.call-done = f32[128,768]{1,0:T(8,128)} async-done(((f32[512,768]{1,0:T(8,128)}), f32[128,768]{1,0:T(8,128)}) %reduce-scatter.7.cloned.1.call-update) | async-done | bytes 393232 | tf_op jit(solution)/shard_map/reduce_scatter | solution.py:53
  177.3 2.3 fusion.33
  180.3 15.2 %all_gather.15 = bf16[512,768]{1,0:T(8,128)(2,1)S(1)} all-gather(bf16[128,768]{1,0:T(8,128)(2,1)S(1)} %convert_element_type.94), channel_id=1, replica_groups=mesh['dp'=8,'tensor'=4] {'tensor'}, dimensions={0}, use_global_device_ids=true | all-gather | bytes 983040 | tf_op jit(solution)/shard_map/all_gather | solution.py:49
  195.9 1.6 convert_reduce_fusion.3
  197.7 1.3 multiply_convert_fusion
  200.7 2.0 fusion.39
  202.8 3.5 convolution_multiply_fusion.1
  206.3 2.4 convolution_multiply_fusion
  208.6 1.1 convolution_multiply_fusion.3
  209.8 1.8 convolution_multiply_fusion.2
  212.5 15.3 %all-reduce.1 = (f32[2,192]{1,0:T(2,128)}, f32[768]{0:T(1024)}) all-reduce(f32[2,192]{1,0:T(2,128)S(1)} %maximum_multiply_fusion, f32[768]{0:T(1024)S(1)} %broadcast_multiply_fusion.1), channel_id=1, replica_groups=mesh['dp'=8,'tensor'=4] {'dp'}, use_global_device_ids=true, to_apply=%region_22.23 | all-reduce | flops 1152 | bytes 9216 | tf_op jit(solution)/shard_map/psum | solution.py:180
  227.8 12.8 %reduce-scatter.11.cloned.1.call-done = f32[128,768]{1,0:T(8,128)} async-done(((f32[512,768]{1,0:T(8,128)}), f32[128,768]{1,0:T(8,128)}) %reduce-scatter.11.cloned.1.call-update) | async-done | bytes 393232 | tf_op jit(solution)/shard_map/reduce_scatter | solution.py:53
  240.6 1.2 fusion.26
  241.8 41.2 %all-reduce = (f32[768]{0:T(1024)}, f32[768]{0:T(1024)}, f32[768]{0:T(1024)}, f32[768]{0:T(1024)}, f32[768]{0:T(1024)}, /*index=5*/f32[768]{0:T(1024)}) all-reduce(f32[768]{0:T(1024)S(1)} %broadcast_multiply_fusion.6, f32[768]{0:T(1024)S(1)} %broadcast_multiply_fusion.5, ...), channel_id=1, replica_groups=mesh['dp'=8,'tensor'=4] {'dp','tensor'}, use_global_device_ids=true, to_apply=%region_16.17 | all-reduce | flops 4608 | bytes 36864 | tf_op jit(solution)/shard_map/psum | solution.py:190
  283.0 1.9 fusion.25
  285.0 74.3 %all-reduce.5.cloned.1.call-done = (f32[768,3,192]{0,2,1:T(8,128)}, f32[192,768]{1,0:T(8,128)}, f32[768,768]{1,0:T(8,128)}, f32[768,768]{1,0:T(8,128)}) async-done(((f32[768,3,192]{0,2,1:T(8,128)}, f32[192,768]{1,0:T(8,128)}, f32[768,768]{1,0:T(8,128)}, f32[768,768]{1,0:T(8,128)}), (f32[768,3,192]{0,2,1:T(8,128)}, f32[192,768]{1,0:T(8,128)}, f32[768,768]{1,0:T(8,128)}, ...) | async-done | bytes 7077904 | tf_op jit(solution)/shard_map/psum | solution.py:180
  359.3 2.9 copy.43
  363.1 1.4 copy.45
  365.6 1.4 copy.46
  (128 shorter events, 13.1 us)
Async XLA Ops:
  7.2 88.9 %copy-start = (bf16[768,768]{1,0:T(8,128)(2,1)S(1)}, bf16[768,768]{1,0:T(8,128)(2,1)}, u32[]{:S(2)}) copy-start(bf16[768,768]{1,0:T(8,128)(2,1)} %param.27) | copy-start | bytes 3538948
  7.2 19.3 %copy-start.36 = (f32[2,192]{1,0:T(2,128)S(1)}, f32[2,192]{1,0:T(2,128)}, u32[]{:S(2)}) copy-start(f32[2,192]{1,0:T(2,128)} %param.20) | copy-start | bytes 4612
  7.2 19.3 %copy-start.25 = (s32[1,512]{1,0:T(1,128)S(1)}, s32[1,512]{1,0:T(1,128)}, u32[]{:S(2)}) copy-start(s32[1,512]{1,0:T(1,128)} %param.16) | copy-start | bytes 6148
  7.2 19.6 %copy-start.15 = (bf16[768,3,192]{0,2,1:T(8,128)(2,1)S(1)}, bf16[768,3,192]{0,2,1:T(8,128)(2,1)}, u32[]{:S(2)}) copy-start(bf16[768,3,192]{0,2,1:T(8,128)(2,1)} %param.19) | copy-start | bytes 2654212
  7.2 71.0 %reduce-scatter.5.cloned.1.call-start = ((), (), s32[]{:S(2)}) async-start(), calls=%async_computation.4 | async-start | bytes 1966080 | tf_op jit(solution)/shard_map/reduce_scatter | solution.py:53
  8.5 18.0 %copy-start.26 = (f32[128]{0:T(128)}, f32[128]{0:T(128)S(1)}, u32[]{:S(2)}) copy-start(f32[128]{0:T(128)S(1)} %broadcast_multiply_fusion.12) | copy-start | bytes 1540
  9.6 16.9 %copy-start.29 = (f32[128]{0:T(128)}, f32[128]{0:T(128)S(1)}, u32[]{:S(2)}) copy-start(f32[128]{0:T(128)S(1)} %add_rsqrt_fusion.1) | copy-start | bytes 1540
  30.9 166.6 %copy-start.10 = (bf16[3,64,512]{2,1,0:T(8,128)(2,1)}, bf16[3,64,512]{2,1,0:T(8,128)(2,1)S(1)}, u32[]{:S(2)}) copy-start(bf16[3,64,512]{2,1,0:T(8,128)(2,1)S(1)} %convolution_convert_fusion.3) | copy-start | bytes 589828
  32.5 45.7 %copy-start.1 = (bf16[128,768]{1,0:T(8,128)(2,1)S(1)}, bf16[128,768]{1,0:T(8,128)(2,1)}, u32[]{:S(2)}) copy-start(bf16[128,768]{1,0:T(8,128)(2,1)} %param.15) | copy-start | bytes 589828
  32.5 45.7 %copy-start.31 = (f32[768]{0:T(1024)S(1)}, f32[768]{0:T(1024)}, u32[]{:S(2)}) copy-start(f32[768]{0:T(1024)} %param.22) | copy-start | bytes 9220
  32.5 47.1 %copy-start.23 = (f32[768]{0:T(1024)S(1)}, f32[768]{0:T(1024)}, u32[]{:S(2)}) copy-start(f32[768]{0:T(1024)} %param.23) | copy-start | bytes 9220
  32.5 47.1 %copy-start.32 = (f32[768]{0:T(1024)S(1)}, f32[768]{0:T(1024)}, u32[]{:S(2)}) copy-start(f32[768]{0:T(1024)} %param.24) | copy-start | bytes 9220
  32.6 107.5 %reduce-scatter.9.cloned.1.call-start = ((), (), s32[]{:S(2)}) async-start(), calls=%async_computation.6 | async-start | bytes 1966080 | tf_op jit(solution)/shard_map/reduce_scatter | solution.py:53
  56.1 39.1 %copy-start.38 = (f32[768]{0:T(1024)S(1)}, f32[768]{0:T(1024)}, u32[]{:S(2)}) copy-start(f32[768]{0:T(1024)} %param.26) | copy-start | bytes 9220
  78.2 17.0 %copy-start.37 = (bf16[768,768]{1,0:T(8,128)(2,1)S(1)}, bf16[768,768]{1,0:T(8,128)(2,1)}, u32[]{:S(2)}) copy-start(bf16[768,768]{1,0:T(8,128)(2,1)} %param.25) | copy-start | bytes 3538948
  96.4 2.9 copy-start.39
  102.4 74.9 %reduce-scatter.7.cloned.1.call-start = ((), (), s32[]{:S(2)}) async-start(), calls=%async_computation.5 | async-start | bytes 1966080 | tf_op jit(solution)/shard_map/reduce_scatter | solution.py:53
  106.1 71.2 %copy-start.33 = (f32[768]{0:T(1024)S(1)}, f32[768]{0:T(1024)}, u32[]{:S(2)}) copy-start(f32[768]{0:T(1024)} %param.28) | copy-start | bytes 9220
  106.1 134.5 %reduce-scatter.11.cloned.1.call-start = ((), (), s32[]{:S(2)}) async-start(), calls=%async_computation.7 | async-start | bytes 1966080 | tf_op jit(solution)/shard_map/reduce_scatter | solution.py:53
  177.3 18.6 %copy-start.5 = (f32[3,512,512]{1,2,0:T(8,128)S(1)}, f32[3,512,512]{1,2,0:T(8,128)}, u32[]{:S(2)}) copy-start(f32[3,512,512]{1,2,0:T(8,128)} %copy-done.4) | copy-start | bytes 9437188
  179.6 16.3 %copy-start.14 = (pred[512,512]{0,1:T(8,128)(4,1)S(1)}, pred[512,512]{0,1:T(8,128)(4,1)}, u32[]{:S(2)}) copy-start(pred[512,512]{0,1:T(8,128)(4,1)} %copy-done.13) | copy-start | bytes 786436
  202.7 156.6 %all-reduce.5.cloned.1.call-start = ((), (), s32[]{:S(2)}) async-start(), calls=%async_computation.8 | async-start | bytes 14155776 | tf_op jit(solution)/shard_map/psum | solution.py:180
  202.7 3.5 copy-start.18
  202.8 3.5 copy-start.40
  206.3 2.4 copy-start.11
  211.6 29.0 %copy-start.24 = (f32[768]{0:T(1024)S(1)}, f32[768]{0:T(1024)}, u32[]{:S(2)}) copy-start(f32[768]{0:T(1024)} %param.17) | copy-start | bytes 9220
  211.6 29.0 %copy-start.27 = (f32[128]{0:T(128)S(1)}, f32[128]{0:T(128)}, u32[]{:S(2)}) copy-start(f32[128]{0:T(128)} %copy-done.26) | copy-start | bytes 1540
  211.6 28.9 %copy-start.30 = (f32[128]{0:T(128)S(1)}, f32[128]{0:T(128)}, u32[]{:S(2)}) copy-start(f32[128]{0:T(128)} %copy-done.29) | copy-start | bytes 1540
  211.6 71.4 %copy-start.3 = (f32[128,768]{1,0:T(8,128)S(1)}, f32[128,768]{1,0:T(8,128)}, u32[]{:S(2)}) copy-start(f32[128,768]{1,0:T(8,128)} %copy-done.2) | copy-start | bytes 1179652
  359.3 3.0 copy-start.20
  359.3 3.8 %copy-start.9 = (f32[768,768]{1,0:T(8,128)S(1)}, f32[768,768]{1,0:T(8,128)}, u32[]{:S(2)}) copy-start(f32[768,768]{1,0:T(8,128)} %get-tuple-element.118) | copy-start | bytes 7077892
  363.1 2.5 copy-start.8
  (14 other events, 17.3 us)
Sparse Core Ops, SparseCore 0:
  32.7 45.5 reduce-scatter.4
  102.5 37.5 reduce-scatter.8
  143.0 34.2 reduce-scatter.6
  202.8 37.7 reduce-scatter.10
  245.3 114.0 all-reduce.4
where the time goes:
time: 376 us; the launch traced here: 374 us
  waiting for transfers between devices  179 us (48%)
  blocking collectives  126 us (34%)
  matrix products  30.1 us (8%)
  between operations  14.2 us (4%)
  other arithmetic  12.9 us (3%)
  local copies, waits for them, and re-layouts  10.7 us (3%)
    reduce_scatter x4, waiting for transfers between devices, scatter_rows(): return lax.psum_scatter(values, 'tensor', scatter_dimension=0, tiled=True)  105 us
    psum x1, waiting for transfers between devices, on_device(): lax.psum((g_qkv_w, g_qv_b, g_out_w, g_proj_w, g_fc_w, g_fc_b), 'dp')  74.3 us
    all_gather x4, blocking collectives, gather_rows(): return lax.all_gather(values, 'tensor', axis=0, tiled=True)  69.8 us
    psum x1, blocking collectives, on_device(): lax.psum((first_norm_gain_gradient, first_norm_bias_gradient, g_out_b, se...  41.2 us
    psum x1, blocking collectives, on_device(): lax.psum((g_qkv_w, g_qv_b, g_out_w, g_proj_w, g_fc_w, g_fc_b), 'dp')  15.3 us
    unnamed x86, local copies, waits for them, and re-layouts  10.5 us
  transfers between devices with their start and end apart: 5, of which 5 were waited for; matrix products, arithmetic and copies ran while one was open for 5% of the time, Pallas kernels for 0%

commit v1 on v0

--- a/solution.py
+++ b/solution.py
@@ -3,6 +3,8 @@
 import jax
 import jax.numpy as jnp
 from jax import lax
+from jax.experimental import pallas as pl
+from jax.experimental.pallas import tpu as pltpu
 from jax.sharding import PartitionSpec as P
 
 HD = 64
@@ -216,9 +218,406 @@
     )
 
 
+NT = 4
+NC = 4
+ROWS = 128
+ORDER = (0, 3, 1, 2)
+MESH = pl.DeviceIdType.MESH
+F32 = jnp.float32
+BF16 = jnp.bfloat16
+
+
+def mm(a, b):
+    return lax.dot_general(a, b, (((1,), (0,)), ((), ())), preferred_element_type=F32)
+
+
+def mm_nt(a, b):
+    return lax.dot_general(a, b, (((1,), (1,)), ((), ())), preferred_element_type=F32)
+
+
+def mm_tn(a, b):
+    return lax.dot_general(a, b, (((0,), (0,)), ((), ())), preferred_element_type=F32)
+
+
+def norm_stats(values):
+    centered = values - jnp.mean(values, axis=-1, keepdims=True)
+    rstd = lax.rsqrt(jnp.mean(centered * centered, axis=-1, keepdims=True) + EPS)
+    return centered * rstd, rstd
+
+
+def norm_back(cot, xhat, rstd, gain):
+    e = cot * gain
+    return rstd * (
+        e
+        - jnp.mean(e, axis=-1, keepdims=True)
+        - xhat * jnp.mean(e * xhat, axis=-1, keepdims=True)
+    )
+
+
+def layer_kernel(
+    x_ref, g_ref, seg_col, seg_row, ln1, wqkv, bqkv, wout, ln2, wfc, bfc, wproj, bproj,
+    bo_out, din_out, grad_out, vec_out,
+    xfull, gfull, wfull, n1, qh, kh, vh, pscr, ofull, mid, n2, act, dpre,
+    bo_send, dn2_send, dn1_send, bo_recv, dn2_recv, dn1_recv, dmid, dmid_own,
+    dkacc, dvacc, dqkv, gl, d2d, hsum, rs, vsend, vbuf, wsend, wbuf,
+    x_s, x_r, g_s, g_r, w1_s, w1_r, w2_s, w2_r, loc_s, o_s, o_r, n2_s, n2_r, n1_s, n1_r,
+    b_s, b_r, m_s, m_r, d1_s, d1_r, rs_s, rs_r, ag_s, ag_r, d2_s, d2_r, va_s, va_r, vb_s, vb_r,
+):
+    d = lax.axis_index("dp")
+    t = lax.axis_index("tensor")
+    chip = d // 2
+    core = d % 2
+
+    def at_t(o):
+        return (d, lax.rem(t + o, NT))
+
+    def at_d(o):
+        return (lax.rem(d + o, 8), t)
+
+    def at_chip(o):
+        return (lax.rem(chip + o, NC) * 2 + core, t)
+
+    sibling = (chip * 2 + 1 - core, t)
+
+    barrier = pltpu.get_barrier_semaphore()
+    for o in range(1, NT):
+        pl.semaphore_signal(barrier, inc=1, device_id=at_t(o), device_id_type=MESH)
+    for o in range(1, 8):
+        pl.semaphore_signal(barrier, inc=1, device_id=at_d(o), device_id_type=MESH)
+    pl.semaphore_wait(barrier, NT - 1 + 7)
+
+    pending = []
+
+    def rcopy(src, dst, ss, rsem, dev):
+        return pltpu.make_async_remote_copy(
+            src_ref=src, dst_ref=dst, send_sem=ss, recv_sem=rsem, device_id=dev, device_id_type=MESH
+        )
+
+    def go(*args):
+        c = rcopy(*args)
+        c.start()
+        pending.append(c)
+        return c
+
+    def rows_of(j):
+        return pl.ds(pl.multiple_of(j * ROWS, ROWS), ROWS)
+
+    cx = [go(x_ref, xfull.at[t], x_s.at[o], x_r.at[o], at_t(o)) for o in range(1, NT)]
+    cols = pl.ds(pl.multiple_of(core * 384, 128), 384)
+    wsrc = wout.at[pl.ds(pl.multiple_of(chip * 48, 16), 48), cols]
+    own_w = pltpu.make_async_copy(wsrc, wfull.at[t, chip, :, cols], loc_s)
+    own_w.start()
+    cw1 = [
+        go(wsrc, wfull.at[t, chip, :, cols], w1_s.at[o], w1_r.at[o], at_t(o))
+        for o in range(1, NT)
+    ]
+    cg = [go(g_ref, gfull.at[t], g_s.at[o], g_r.at[o], at_t(o)) for o in range(1, NT)]
+    xfull[t] = x_ref[...]
+    gfull[t] = g_ref[...]
+
+    for o in range(NT):
+        if o:
+            cx[o - 1].wait_recv()
+        s = lax.rem(t + NT - o, NT)
+        xhat, _ = norm_stats(xfull[s].astype(F32))
+        nb = (xhat * ln1[0:1, :] + ln1[1:2, :]).astype(BF16)
+        n1[rows_of(s), :] = nb
+        qkv = (mm(nb, wqkv[...]) + bqkv[...]).astype(BF16)
+        for h in range(3):
+            qh[h, rows_of(s), :] = qkv[:, h * HD : h * HD + HD]
+            kh[h, rows_of(s), :] = qkv[:, 192 + h * HD : 192 + h * HD + HD]
+            vh[h, rows_of(s), :] = qkv[:, 384 + h * HD : 384 + h * HD + HD]
+
+    own_w.wait()
+    for c in cw1:
+        c.wait_recv()
+    wpart = wfull.at[:, chip, :, cols]
+    cw2 = [go(wpart, wpart, w2_s.at[o], w2_r.at[o], at_d(o)) for o in range(1, 8)]
+
+    co = {}
+    for j in ORDER:
+        r = slice(j * ROWS, (j + 1) * ROWS)
+        n = (j + 1) * ROWS
+        qi = j * ROWS + lax.broadcasted_iota(jnp.int32, (ROWS, n), 0)
+        ki = lax.broadcasted_iota(jnp.int32, (ROWS, n), 1)
+        allowed = (seg_col[r, :] == seg_row[:, :n]) & (qi >= ki)
+        outs = []
+        for h in range(3):
+            sc = jnp.where(allowed, mm_nt(qh[h, r, :], kh[h, :n, :]) * 0.125, -1e30)
+            e = jnp.exp(sc - jnp.max(sc, axis=-1, keepdims=True))
+            p = e * (1.0 / jnp.sum(e, axis=-1, keepdims=True))
+            pscr[h, r, :n] = p
+            outs.append(mm(p.astype(BF16), vh[h, :n, :]))
+        ofull[t, r, :] = jnp.concatenate(outs, axis=1).astype(BF16)
+        co[j] = [
+            go(ofull.at[t, r], ofull.at[t, r], o_s.at[j, o], o_r.at[j, o], at_t(o))
+            for o in range(1, NT)
+        ]
+
+    for c in cw2:
+        c.wait_recv()
+    for c in cg:
+        c.wait_recv()
+
+    def send_block(buf, recv, ss, rsem, j):
+        o = lax.rem(j - t + NT, NT)
+        return rcopy(buf.at[j], recv.at[o], ss.at[j], rsem.at[o], (d, j))
+
+    for j in ORDER:
+        r = slice(j * ROWS, (j + 1) * ROWS)
+        for c in co[j]:
+            c.wait_recv()
+        m = xfull[j].astype(F32) + ln2[2:3, :]
+        for s in range(NT):
+            m = m + mm(ofull[s, r, :], wfull[s].reshape(192, 768))
+        mid[r, :] = m
+        xhat, _ = norm_stats(m)
+        nb = (xhat * ln2[0:1, :] + ln2[1:2, :]).astype(BF16)
+        n2[r, :] = nb
+        pre = mm(nb, wfc[...]) + bfc[...]
+        sq = pre * pre
+        tangent = jnp.tanh(GELU_C * (pre + 0.044715 * (sq * pre)))
+        slope = 0.5 * (1.0 + tangent) + 0.5 * pre * (1.0 - tangent * tangent) * GELU_C * (
+            1.0 + 3.0 * 0.044715 * sq
+        )
+        ab = (0.5 * pre * (1.0 + tangent)).astype(BF16)
+        act[r, :] = ab
+        dp = (mm_nt(gfull[j], wproj[...]) * slope).astype(BF16)
+        dpre[r, :] = dp
+        dn2_send[j] = mm_nt(dp, wfc[...]).astype(BF16)
+
+        @pl.when(t != j)
+        def _():
+            send_block(dn2_send, dn2_recv, n2_s, n2_r, j).start()
+
+        bo_send[j] = mm(ab, wproj[...]).astype(BF16)
+
+    def stage1(i):
+        half = pl.ds(pl.multiple_of((1 - core) * 384, 128), 384)
+        return go(gl.at[i, half], d2d.at[i], d1_s.at[i], d1_r.at[i], sibling)
+
+    def stage2(i, c):
+        c.wait_recv()
+        half = pl.ds(pl.multiple_of(core * 384, 128), 384)
+        hsum[i] = (gl[i, half, :].astype(F32) + d2d[i].astype(F32)).astype(BF16)
+        out = []
+        for o in range(1, NC):
+            to = pl.ds(pl.multiple_of(lax.rem(chip + o, NC) * 96, 32), 96)
+            out.append(go(hsum.at[i, to], rs.at[i, o], rs_s.at[i, o], rs_r.at[i, o], at_chip(o)))
+        return out
+
+    def stage3(i, cs):
+        own = pl.ds(pl.multiple_of(chip * 96, 32), 96)
+        total = hsum[i, own, :].astype(F32)
+        for o in range(1, NC):
+            cs[o - 1].wait_recv()
+            total = total + rs[i, o].astype(F32)
+        at = pl.ds(pl.multiple_of(core * 384 + chip * 96, 32), 96)
+        grad_out[i, at, :] = total.astype(BF16)
+        blk = grad_out.at[i, at]
+        return [
+            go(blk, blk, ag_s.at[i, o], ag_r.at[i, o], at_chip(o)) for o in range(1, NC)
+        ]
+
+    def stage4(i, cs):
+        for c in cs:
+            c.wait_recv()
+        half = grad_out.at[i, pl.ds(pl.multiple_of(core * 384, 128), 384)]
+        return go(half, half, d2_s.at[i], d2_r.at[i], sibling)
+
+    gmat = gfull[...].reshape(NT * ROWS, 768)
+    gl[0] = mm_tn(act[...], gmat).astype(BF16)
+    c1a = stage1(0)
+    gl[1] = mm_tn(n2[...], dpre[...]).astype(BF16)
+    c1b = stage1(1)
+
+    def gathered(send, recv, ss, rsem):
+        total = send[t].astype(F32)
+        for o in range(1, NT):
+            rcopy(send.at[0], recv.at[o], ss.at[0], rsem.at[o], at_t(o)).wait_recv()
+            total = total + recv[o].astype(F32)
+        return total
+
+    own_rows = rows_of(t)
+    gown = g_ref[...].astype(F32)
+    dn2 = gathered(dn2_send, dn2_recv, n2_s, n2_r)
+    xhat, rstd = norm_stats(mid[own_rows, :])
+    dm = gown + norm_back(dn2, xhat, rstd, ln2[0:1, :])
+    dmid_own[...] = dm
+    dmid[t] = dm.astype(BF16)
+    for o in range(1, NT):
+        go(dmid.at[t], dmid.at[t], m_s.at[o], m_r.at[o], at_t(o))
+    vsend[2:3, :] = jnp.sum(dm, axis=0, keepdims=True)
+    vsend[3:4, :] = jnp.sum(dn2 * xhat, axis=0, keepdims=True)
+    vsend[4:5, :] = jnp.sum(dn2, axis=0, keepdims=True)
+    vsend[5:6, :] = jnp.sum(gown, axis=0, keepdims=True)
+    vsend[6:7, :] = jnp.sum(dpre[...].astype(F32), axis=0, keepdims=True)
+    for j in ORDER:
+
+        @pl.when(t != j)
+        def _():
+            send_block(bo_send, bo_recv, b_s, b_r, j).start()
+
+    c2a = stage2(0, c1a)
+    c2b = stage2(1, c1b)
+
+    dkacc[...] = jnp.zeros_like(dkacc)
+    dvacc[...] = jnp.zeros_like(dvacc)
+    for j in (3, 2, 1, 0):
+        r = slice(j * ROWS, (j + 1) * ROWS)
+        n = (j + 1) * ROWS
+
+        @pl.when(t != j)
+        def _():
+            o = lax.rem(t - j + NT, NT)
+            rcopy(dmid.at[j], dmid.at[j], m_s.at[o], m_r.at[o], (d, j)).wait_recv()
+
+        do = mm_nt(dmid[j], wout[...]).astype(BF16)
+        ob = ofull[t, r, :].astype(F32) * do.astype(F32)
+        dq = []
+        for h in range(3):
+            hs = slice(h * HD, h * HD + HD)
+            doh = do[:, hs]
+            p = pscr[h, r, :n]
+            dvacc[h, :n, :] += mm_tn(p.astype(BF16), doh)
+            delta = jnp.sum(ob[:, hs], axis=-1, keepdims=True)
+            ds = (p * (mm_nt(doh, vh[h, :n, :]) - delta) * 0.125).astype(BF16)
+            dq.append(mm(ds, kh[h, :n, :]))
+            dkacc[h, :n, :] += mm_tn(ds, qh[h, r, :])
+        parts = dq + [dkacc[h, r, :] for h in range(3)] + [dvacc[h, r, :] for h in range(3)]
+        dqkv[r, :] = jnp.concatenate(parts, axis=1).astype(BF16)
+        dn1_send[j] = mm_nt(dqkv[r, :], wqkv[...]).astype(BF16)
+
+        @pl.when(t != j)
+        def _():
+            send_block(dn1_send, dn1_recv, n1_s, n1_r, j).start()
+
+        if j == 1:
+            c3a = stage3(0, c2a)
+            c3b = stage3(1, c2b)
+
+    gl[2, :, 0:576] = mm_tn(n1[...], dqkv[...]).astype(BF16)
+    dmat = dmid[...].reshape(NT * ROWS, 768)
+    gl[2, :, 576:768] = mm_tn(dmat, ofull[t]).astype(BF16)
+    c1c = stage1(2)
+    dsum = jnp.sum(dqkv[...].astype(F32), axis=0, keepdims=True)
+    vsend[7:8, :] = jnp.concatenate([dsum, jnp.zeros((1, 192), F32)], axis=1)
+    c4a = stage4(0, c3a)
+    c4b = stage4(1, c3b)
+    c2c = stage2(2, c1c)
+    bo = gathered(bo_send, bo_recv, b_s, b_r)
+    bo_out[...] = mid[own_rows, :] + bo + bproj[...]
+    dn1 = gathered(dn1_send, dn1_recv, n1_s, n1_r)
+    xhat, rstd = norm_stats(x_ref[...].astype(F32))
+    din_out[...] = dmid_own[...] + norm_back(dn1, xhat, rstd, ln1[0:1, :])
+    vsend[0:1, :] = jnp.sum(dn1 * xhat, axis=0, keepdims=True)
+    vsend[1:2, :] = jnp.sum(dn1, axis=0, keepdims=True)
+    cva = [go(vsend, vbuf.at[t], va_s.at[o], va_r.at[o], at_t(o)) for o in range(1, NT)]
+    vbuf[t] = vsend[...]
+    c3c = stage3(2, c2c)
+    for c in cva:
+        c.wait_recv()
+    wsend[...] = ((vbuf[0] + vbuf[1]) + vbuf[2]) + vbuf[3]
+    wsend[6:8, :] = vsend[6:8, :]
+    cvb = [go(wsend, wbuf.at[d], vb_s.at[o], vb_r.at[o], at_d(o)) for o in range(1, 8)]
+    wbuf[d] = wsend[...]
+    c4c = stage4(2, c3c)
+    for c in cvb:
+        c.wait_recv()
+    total = wbuf[0]
+    for s in range(1, 8):
+        total = total + wbuf[s]
+    vec_out[...] = total * 0.125
+    c4a.wait_recv()
+    c4b.wait_recv()
+    c4c.wait_recv()
+
+    for c in pending:
+        c.wait_send()
+    for j in range(NT):
+
+        @pl.when(t != j)
+        def _():
+            send_block(dn2_send, dn2_recv, n2_s, n2_r, j).wait_send()
+            send_block(bo_send, bo_recv, b_s, b_r, j).wait_send()
+            send_block(dn1_send, dn1_recv, n1_s, n1_r, j).wait_send()
+
+
+def on_device_fused(
+    block_in, segment_ids, first_norm_gain, first_norm_bias, qkv_weight, qv_bias, out_weight,
+    out_bias, second_norm_gain, second_norm_bias, fc_weight, fc_bias, proj_weight, proj_bias,
+    out_grad,
+):
+    wqkv = qkv_weight.reshape(768, 576)
+    bqkv = jnp.concatenate([qv_bias[0], jnp.zeros_like(qv_bias[0]), qv_bias[1]])[None]
+    ln1 = jnp.stack([first_norm_gain, first_norm_bias])
+    ln2 = jnp.stack([second_norm_gain, second_norm_bias, out_bias])
+    full = lambda dt: pltpu.VMEM((NT, ROWS, 768), dt)
+    head = lambda dt: pltpu.VMEM((3, 512, HD), dt)
+    tall = lambda n, dt: pltpu.VMEM((512, n), dt)
+    dma = lambda *s: pltpu.SemaphoreType.DMA(s)
+    scratch = [
+        full(BF16), full(BF16), pltpu.VMEM((NT, NC, 48, 768), BF16), tall(768, BF16),
+        head(BF16), head(BF16), head(BF16), pltpu.VMEM((3, 512, 512), F32),
+        pltpu.VMEM((NT, 512, 192), BF16), tall(768, F32), tall(768, BF16), tall(768, BF16),
+        tall(768, BF16),
+        full(BF16), full(BF16), full(BF16), full(BF16), full(BF16), full(BF16), full(BF16),
+        pltpu.VMEM((ROWS, 768), F32),
+        head(F32), head(F32), tall(576, BF16),
+        pltpu.VMEM((3, 768, 768), BF16), pltpu.VMEM((3, 384, 768), BF16),
+        pltpu.VMEM((3, 384, 768), BF16), pltpu.VMEM((3, NC, 96, 768), BF16),
+        pltpu.VMEM((8, 768), F32), pltpu.VMEM((NT, 8, 768), F32),
+        pltpu.VMEM((8, 768), F32), pltpu.VMEM((8, 8, 768), F32),
+        dma(4), dma(4), dma(4), dma(4), dma(4), dma(4), dma(8), dma(8), pltpu.SemaphoreType.DMA,
+        dma(4, 4), dma(4, 4), dma(4), dma(4), dma(4), dma(4), dma(4), dma(4), dma(4), dma(4),
+        dma(3), dma(3), dma(3, 4), dma(3, 4), dma(3, 4), dma(3, 4), dma(3), dma(3),
+        dma(4), dma(4), dma(8), dma(8),
+    ]
+    vm = pl.BlockSpec(memory_space=pltpu.VMEM)
+    block_out, d_in, grads, vecs = pl.pallas_call(
+        layer_kernel,
+        out_shape=(
+            jax.ShapeDtypeStruct((ROWS, 768), F32),
+            jax.ShapeDtypeStruct((ROWS, 768), F32),
+            jax.ShapeDtypeStruct((3, 768, 768), BF16),
+            jax.ShapeDtypeStruct((8, 768), F32),
+        ),
+        in_specs=[vm] * 13,
+        out_specs=[vm] * 4,
+        scratch_shapes=scratch,
+        compiler_params=pltpu.CompilerParams(
+            collective_id=0, has_side_effects=True, vmem_limit_bytes=60 * 1024 * 1024
+        ),
+        cost_estimate=pl.CostEstimate(
+            flops=8_000_000_000, bytes_accessed=12_000_000, transcendentals=2_000_000
+        ),
+    )(
+        block_in, out_grad, segment_ids.reshape(512, 1), segment_ids, ln1, wqkv, bqkv, out_weight,
+        ln2, fc_weight, fc_bias[None], proj_weight, proj_bias[None],
+    )
+    scaled = lambda a: a.astype(F32) * 0.125
+    return (
+        block_out,
+        d_in,
+        vecs[0],
+        vecs[1],
+        scaled(grads[2, :, :576]).reshape(768, 3, 192),
+        jnp.stack([vecs[7, :192], vecs[7, 384:576]]),
+        scaled(grads[2, :, 576:]).T,
+        vecs[2],
+        vecs[3],
+        vecs[4],
+        scaled(grads[1]),
+        vecs[6],
+        scaled(grads[0]),
+        vecs[5],
+    )
+
+
 def solution(mesh):
+    fits = mesh.shape["dp"] == 8 and mesh.shape["tensor"] == 4
     return jax.shard_map(
-        on_device,
+        on_device_fused if fits else on_device,
         mesh=mesh,
         in_specs=(
             P(("dp", "tensor"), None),

time: 376 us -> 187 us (0.50)
  the two profiles are of different devices: /device:TPU:17 before, /device:TPU:25 now
where the time goes in v1:
time: 187 us; the launch traced here: 186 us
  Pallas kernels  159 us (85%)
  local copies, waits for them, and re-layouts  17.7 us (9%)
  other arithmetic  8.63 us (5%)
    pallas_call x1, Pallas kernels, on_device_fused(): pl.pallas_call(layer_kernel, out_shape=(jax.ShapeDtypeStruct((ROWS, 768),...  159 us
    mul x2, other arithmetic, on_device_fused(): scaled = lambda a: a.astype(F32) * 0.125  5.57 us

profile of v1, /device:TPU:25, one launch (start us, length us, event | category | flops | bytes accessed | tf_op | source)
XLA Modules:
  0.0 186.0 jit_solution(13309676669663465946)
XLA Ops:
  0.6 0.8 fusion.1
  1.4 0.1 pad_maximum_fusion.2
  1.5 0.6 broadcast_in_dim.13.bqkv
  2.1 0.7 stack.24
  2.8 0.7 stack.25
  3.4 0.6 pad_maximum_fusion.1.ln1
  4.1 0.7 stack.29
  4.7 0.7 stack.27
  5.4 0.7 stack.28
  6.1 0.6 pad_maximum_fusion.ln2
  6.7 1.3 broadcast_in_dim.14.bfc
  8.0 1.3 broadcast_in_dim.15.bproj
  9.3 1.5 copy.36.seg_col
  10.8 2.2 %copy.37.wqkv = bf16[768,576]{1,0:T(8,128)(2,1)} copy(bf16[768,576]{0,1:T(8,128)(2,1)} %bitcast.14) | data formatting | bytes 1769472 | tf_op jit(solution)/shard_map/reshape | solution.py:551
  13.0 158.9 %shard_map.254 = (f32[128,768]{1,0:T(8,128)}, f32[128,768]{1,0:T(8,128)}, bf16[3,768,768]{2,1,0:T(8,128)(2,1)}, f32[8,768]{1,0:T(8,128)}) custom-call(bf16[128,768]{1,0:T(8,128)(2,1)} %x_ref.1, bf16[128,768]{1,0:T(8,128)(2,1)} %g_ref.1, s32[512,1]{1,0:T(8,128)} %copy.36.seg_col, s32[1,512]{1,0:T(1,128)} %seg_row.1, f32[2,768]{1,0:T(2,128)} %pad_maximum_fusion.1.ln1, ...), custom_call_target="tpu_custom_call" | custom-call | flops 8000000000 | bytes 12000000 | tf_op jit(solution)/shard_map/pallas_call | solution.py:577
  172.0 0.7 fusion
  172.7 0.6 pad_maximum_fusion.3
  173.3 1.7 slice_reduce_fusion
  174.9 1.2 multiply_bitcast_fusion.2
  176.1 1.1 copy.39
  177.2 1.3 convert_multiply_fusion
  178.5 1.7 copy.38
  180.2 0.0 copy-start.1
  180.2 0.0 copy-start
  180.2 4.2 %multiply_bitcast_fusion = (f32[768,768]{1,0:T(8,128)}, f32[768,768]{1,0:T(8,128)}) fusion(bf16[3,768,768]{2,1,0:T(8,128)(2,1)} %get-tuple-element.21), kind=kLoop, calls=%fused_computation | loop fusion | flops 2359296 | bytes 7077888 | tf_op jit(solution)/shard_map/mul | solution.py:598
  184.5 0.0 copy-done.1
  184.5 0.7 copy.42
  185.2 0.0 copy-done
  185.2 0.7 copy.43
  (1 shorter events, 0.0 us)
Async XLA Ops:
  180.2 4.2 %copy-start.1 = (f32[128,768]{1,0:T(8,128)S(1)}, f32[128,768]{1,0:T(8,128)}, u32[]{:S(2)}) copy-start(f32[128,768]{1,0:T(8,128)} %get-tuple-element.91) | copy-start | bytes 1179652
  180.2 5.0 %copy-start = (f32[128,768]{1,0:T(8,128)S(1)}, f32[128,768]{1,0:T(8,128)}, u32[]{:S(2)}) copy-start(f32[128,768]{1,0:T(8,128)} %get-tuple-element.92) | copy-start | bytes 1179652

commit v2 on v1

--- a/solution.py
+++ b/solution.py
@@ -222,6 +222,7 @@
 NC = 4
 ROWS = 128
 ORDER = (0, 3, 1, 2)
+BACK = (3, 2, 1, 0)
 MESH = pl.DeviceIdType.MESH
 F32 = jnp.float32
 BF16 = jnp.bfloat16
@@ -255,8 +256,8 @@
 
 
 def layer_kernel(
-    x_ref, g_ref, seg_col, seg_row, ln1, wqkv, bqkv, wout, ln2, wfc, bfc, wproj, bproj,
-    bo_out, din_out, grad_out, vec_out,
+    x_ref, g_ref, seg_row, gain1, shift1, wqkv, qvb, wout, bout, gain2, shift2, wfc, bfc, wproj, bproj,
+    bo_out, din_out, grad_out, vec_out, qv_out,
     xfull, gfull, wfull, n1, qh, kh, vh, pscr, ofull, mid, n2, act, dpre,
     bo_send, dn2_send, dn1_send, bo_recv, dn2_recv, dn1_recv, dmid, dmid_own,
     dkacc, dvacc, dqkv, gl, d2d, hsum, rs, vsend, vbuf, wsend, wbuf,
@@ -287,6 +288,12 @@
     pl.semaphore_wait(barrier, NT - 1 + 7)
 
     pending = []
+    ln1 = (gain1[...][None], shift1[...][None])
+    ln2 = (gain2[...][None], shift2[...][None], bout[...][None])
+    bqkv = jnp.concatenate([qvb[0:1, :], jnp.zeros((1, 192), F32), qvb[1:2, :]], axis=1)
+    bfc_row = bfc[...][None]
+    seg_col = jnp.transpose(jnp.broadcast_to(seg_row[...].astype(F32), (ROWS, 512)))[:, 0:1]
+    seg_line = seg_row[...].astype(F32)
 
     def rcopy(src, dst, ss, rsem, dev):
         return pltpu.make_async_remote_copy(
@@ -302,7 +309,81 @@
     def rows_of(j):
         return pl.ds(pl.multiple_of(j * ROWS, ROWS), ROWS)
 
-    cx = [go(x_ref, xfull.at[t], x_s.at[o], x_r.at[o], at_t(o)) for o in range(1, NT)]
+    def hop_send(k, ref, ss, rsem, r=None):
+        def go_to(cond, slot, side, to):
+            @pl.when(cond)
+            def _():
+                b = ref.at[slot] if r is None else ref.at[slot, r]
+                rcopy(b, b, ss.at[side, k], rsem.at[side, k], (d, to)).start()
+
+        go_to((t < NT - 1) & (t >= k), t - k, 0, t + 1)
+        go_to((t > 0) & (t + k < NT), t + k, 1, t - 1)
+
+    def hop_wait(k, ref, ss, rsem, r=None):
+        b = ref.at[0] if r is None else ref.at[0, r]
+
+        @pl.when(t >= k + 1)
+        def _():
+            rcopy(b, b, ss.at[0, k], rsem.at[0, k], at_t(1)).wait_recv()
+
+        @pl.when(t + k + 1 < NT)
+        def _():
+            rcopy(b, b, ss.at[1, k], rsem.at[1, k], at_t(1)).wait_recv()
+
+    def hop_sent(ref, ss, rsem, r=None):
+        b = ref.at[0] if r is None else ref.at[0, r]
+        for k in range(NT - 1):
+
+            @pl.when((t < NT - 1) & (t >= k))
+            def _():
+                rcopy(b, b, ss.at[0, k], rsem.at[0, k], at_t(1)).wait_send()
+
+            @pl.when((t > 0) & (t + k < NT))
+            def _():
+                rcopy(b, b, ss.at[1, k], rsem.at[1, k], at_t(1)).wait_send()
+
+    def sum_hop(k, j, send, recv, ss, rsem):
+        for side, here, to in ((0, k, 1), (1, NT - 1 - k, -1)):
+            if (here < j) if side == 0 else (here > j):
+
+                @pl.when(t == here)
+                def _():
+                    c = rcopy(
+                        send.at[j], recv.at[side, j], ss.at[j], rsem.at[side, j], (d, here + to)
+                    )
+                    if k:
+                        c.wait_recv()
+                        send[j] = (send[j].astype(F32) + recv[side, j].astype(F32)).astype(BF16)
+                    c.start()
+
+    def sum_steps(i, order, *bufs):
+        for k in range(NT - 1):
+            if 0 <= i - k < NT:
+                sum_hop(k, order[i - k], *bufs)
+
+    def sum_ends(recv):
+        @pl.when(t == 0)
+        def _():
+            recv[0, 0] = jnp.zeros((ROWS, 768), BF16)
+
+        @pl.when(t == NT - 1)
+        def _():
+            recv[1, NT - 1] = jnp.zeros((ROWS, 768), BF16)
+
+    def gathered(send, recv, ss, rsem):
+        @pl.when(t > 0)
+        def _():
+            rcopy(send.at[t], recv.at[0, t], ss.at[t], rsem.at[0, t], at_t(1)).wait_recv()
+
+        @pl.when(t < NT - 1)
+        def _():
+            rcopy(send.at[t], recv.at[1, t], ss.at[t], rsem.at[1, t], at_t(1)).wait_recv()
+
+        return send[t].astype(F32) + recv[0, t].astype(F32) + recv[1, t].astype(F32)
+
+    xfull[t] = x_ref[...]
+    gfull[t] = g_ref[...]
+    hop_send(0, xfull, x_s, x_r)
     cols = pl.ds(pl.multiple_of(core * 384, 128), 384)
     wsrc = wout.at[pl.ds(pl.multiple_of(chip * 48, 16), 48), cols]
     own_w = pltpu.make_async_copy(wsrc, wfull.at[t, chip, :, cols], loc_s)
@@ -311,36 +392,55 @@
         go(wsrc, wfull.at[t, chip, :, cols], w1_s.at[o], w1_r.at[o], at_t(o))
         for o in range(1, NT)
     ]
-    cg = [go(g_ref, gfull.at[t], g_s.at[o], g_r.at[o], at_t(o)) for o in range(1, NT)]
-    xfull[t] = x_ref[...]
-    gfull[t] = g_ref[...]
-
-    for o in range(NT):
-        if o:
-            cx[o - 1].wait_recv()
-        s = lax.rem(t + NT - o, NT)
+    for buf in (bo_recv, dn2_recv, dn1_recv):
+        sum_ends(buf)
+
+    def project(s):
         xhat, _ = norm_stats(xfull[s].astype(F32))
-        nb = (xhat * ln1[0:1, :] + ln1[1:2, :]).astype(BF16)
+        nb = (xhat * ln1[0] + ln1[1]).astype(BF16)
         n1[rows_of(s), :] = nb
-        qkv = (mm(nb, wqkv[...]) + bqkv[...]).astype(BF16)
+        qkv = (mm_nt(nb, wqkv[...]) + bqkv).astype(BF16)
         for h in range(3):
             qh[h, rows_of(s), :] = qkv[:, h * HD : h * HD + HD]
             kh[h, rows_of(s), :] = qkv[:, 192 + h * HD : 192 + h * HD + HD]
             vh[h, rows_of(s), :] = qkv[:, 384 + h * HD : 384 + h * HD + HD]
 
+    project(t)
+    hop_wait(0, xfull, x_s, x_r)
+    hop_send(1, xfull, x_s, x_r)
+    near = t + 1 - 2 * lax.rem(t, 2)
+    project(near)
+    hop_wait(1, xfull, x_s, x_r)
+    hop_send(2, xfull, x_s, x_r)
+    hop_send(0, gfull, g_s, g_r)
     own_w.wait()
     for c in cw1:
         c.wait_recv()
     wpart = wfull.at[:, chip, :, cols]
+    hop_wait(2, xfull, x_s, x_r)
+    far = lax.rem(t + 2, NT)
+    project(far)
+    project(far + 1 - 2 * lax.rem(far, 2))
+    hop_wait(0, gfull, g_s, g_r)
+    hop_send(1, gfull, g_s, g_r)
     cw2 = [go(wpart, wpart, w2_s.at[o], w2_r.at[o], at_d(o)) for o in range(1, 8)]
 
-    co = {}
-    for j in ORDER:
+    def o_hops(i):
+        for k in range(NT):
+            if 0 <= i - k < NT:
+                j = ORDER[i - k]
+                args = (ofull, o_s.at[j], o_r.at[j], slice(j * ROWS, (j + 1) * ROWS))
+                if k:
+                    hop_wait(k - 1, *args)
+                if k < NT - 1:
+                    hop_send(k, *args)
+
+    for i, j in enumerate(ORDER):
         r = slice(j * ROWS, (j + 1) * ROWS)
         n = (j + 1) * ROWS
         qi = j * ROWS + lax.broadcasted_iota(jnp.int32, (ROWS, n), 0)
         ki = lax.broadcasted_iota(jnp.int32, (ROWS, n), 1)
-        allowed = (seg_col[r, :] == seg_row[:, :n]) & (qi >= ki)
+        allowed = (seg_col[r, :] == seg_line[:, :n]) & (qi >= ki)
         outs = []
         for h in range(3):
             sc = jnp.where(allowed, mm_nt(qh[h, r, :], kh[h, :n, :]) * 0.125, -1e30)
@@ -349,32 +449,30 @@
             pscr[h, r, :n] = p
             outs.append(mm(p.astype(BF16), vh[h, :n, :]))
         ofull[t, r, :] = jnp.concatenate(outs, axis=1).astype(BF16)
-        co[j] = [
-            go(ofull.at[t, r], ofull.at[t, r], o_s.at[j, o], o_r.at[j, o], at_t(o))
-            for o in range(1, NT)
-        ]
+        o_hops(i)
+        if i == 1:
+            hop_wait(1, gfull, g_s, g_r)
+            hop_send(2, gfull, g_s, g_r)
 
     for c in cw2:
         c.wait_recv()
-    for c in cg:
-        c.wait_recv()
-
-    def send_block(buf, recv, ss, rsem, j):
-        o = lax.rem(j - t + NT, NT)
-        return rcopy(buf.at[j], recv.at[o], ss.at[j], rsem.at[o], (d, j))
-
-    for j in ORDER:
+    hop_wait(2, gfull, g_s, g_r)
+
+    dn2_sum = (dn2_send, dn2_recv, n2_s, n2_r)
+    bo_sum = (bo_send, bo_recv, b_s, b_r)
+    dn1_sum = (dn1_send, dn1_recv, n1_s, n1_r)
+    for i, j in enumerate(ORDER):
         r = slice(j * ROWS, (j + 1) * ROWS)
-        for c in co[j]:
-            c.wait_recv()
-        m = xfull[j].astype(F32) + ln2[2:3, :]
+        if i:
+            o_hops(i + 3)
+        m = xfull[j].astype(F32) + ln2[2]
         for s in range(NT):
             m = m + mm(ofull[s, r, :], wfull[s].reshape(192, 768))
         mid[r, :] = m
         xhat, _ = norm_stats(m)
-        nb = (xhat * ln2[0:1, :] + ln2[1:2, :]).astype(BF16)
+        nb = (xhat * ln2[0] + ln2[1]).astype(BF16)
         n2[r, :] = nb
-        pre = mm(nb, wfc[...]) + bfc[...]
+        pre = mm(nb, wfc[...]) + bfc_row
         sq = pre * pre
         tangent = jnp.tanh(GELU_C * (pre + 0.044715 * (sq * pre)))
         slope = 0.5 * (1.0 + tangent) + 0.5 * pre * (1.0 - tangent * tangent) * GELU_C * (
@@ -386,10 +484,7 @@
         dpre[r, :] = dp
         dn2_send[j] = mm_nt(dp, wfc[...]).astype(BF16)
 
-        @pl.when(t != j)
-        def _():
-            send_block(dn2_send, dn2_recv, n2_s, n2_r, j).start()
-
+        sum_steps(i, ORDER, *dn2_sum)
         bo_send[j] = mm(ab, wproj[...]).astype(BF16)
 
     def stage1(i):
@@ -425,52 +520,44 @@
         half = grad_out.at[i, pl.ds(pl.multiple_of(core * 384, 128), 384)]
         return go(half, half, d2_s.at[i], d2_r.at[i], sibling)
 
+    sum_steps(4, ORDER, *dn2_sum)
     gmat = gfull[...].reshape(NT * ROWS, 768)
     gl[0] = mm_tn(act[...], gmat).astype(BF16)
     c1a = stage1(0)
-    gl[1] = mm_tn(n2[...], dpre[...]).astype(BF16)
-    c1b = stage1(1)
-
-    def gathered(send, recv, ss, rsem):
-        total = send[t].astype(F32)
-        for o in range(1, NT):
-            rcopy(send.at[0], recv.at[o], ss.at[0], rsem.at[o], at_t(o)).wait_recv()
-            total = total + recv[o].astype(F32)
-        return total
+    sum_steps(5, ORDER, *dn2_sum)
 
     own_rows = rows_of(t)
     gown = g_ref[...].astype(F32)
-    dn2 = gathered(dn2_send, dn2_recv, n2_s, n2_r)
+    dn2 = gathered(*dn2_sum)
     xhat, rstd = norm_stats(mid[own_rows, :])
-    dm = gown + norm_back(dn2, xhat, rstd, ln2[0:1, :])
+    dm = gown + norm_back(dn2, xhat, rstd, ln2[0])
     dmid_own[...] = dm
     dmid[t] = dm.astype(BF16)
-    for o in range(1, NT):
-        go(dmid.at[t], dmid.at[t], m_s.at[o], m_r.at[o], at_t(o))
+    hop_send(0, dmid, m_s, m_r)
+    sum_steps(0, ORDER, *bo_sum)
+    sum_steps(1, ORDER, *bo_sum)
     vsend[2:3, :] = jnp.sum(dm, axis=0, keepdims=True)
     vsend[3:4, :] = jnp.sum(dn2 * xhat, axis=0, keepdims=True)
     vsend[4:5, :] = jnp.sum(dn2, axis=0, keepdims=True)
     vsend[5:6, :] = jnp.sum(gown, axis=0, keepdims=True)
     vsend[6:7, :] = jnp.sum(dpre[...].astype(F32), axis=0, keepdims=True)
-    for j in ORDER:
-
-        @pl.when(t != j)
-        def _():
-            send_block(bo_send, bo_recv, b_s, b_r, j).start()
-
+    hop_wait(0, dmid, m_s, m_r)
+    hop_send(1, dmid, m_s, m_r)
+    gl[1] = mm_tn(n2[...], dpre[...]).astype(BF16)
+    c1b = stage1(1)
     c2a = stage2(0, c1a)
+    hop_wait(1, dmid, m_s, m_r)
+    hop_send(2, dmid, m_s, m_r)
     c2b = stage2(1, c1b)
+    sum_steps(2, ORDER, *bo_sum)
+    sum_steps(3, ORDER, *bo_sum)
+    hop_wait(2, dmid, m_s, m_r)
 
     dkacc[...] = jnp.zeros_like(dkacc)
     dvacc[...] = jnp.zeros_like(dvacc)
-    for j in (3, 2, 1, 0):
+    for i, j in enumerate(BACK):
         r = slice(j * ROWS, (j + 1) * ROWS)
         n = (j + 1) * ROWS
-
-        @pl.when(t != j)
-        def _():
-            o = lax.rem(t - j + NT, NT)
-            rcopy(dmid.at[j], dmid.at[j], m_s.at[o], m_r.at[o], (d, j)).wait_recv()
 
         do = mm_nt(dmid[j], wout[...]).astype(BF16)
         ob = ofull[t, r, :].astype(F32) * do.astype(F32)
@@ -486,30 +573,30 @@
             dkacc[h, :n, :] += mm_tn(ds, qh[h, r, :])
         parts = dq + [dkacc[h, r, :] for h in range(3)] + [dvacc[h, r, :] for h in range(3)]
         dqkv[r, :] = jnp.concatenate(parts, axis=1).astype(BF16)
-        dn1_send[j] = mm_nt(dqkv[r, :], wqkv[...]).astype(BF16)
-
-        @pl.when(t != j)
-        def _():
-            send_block(dn1_send, dn1_recv, n1_s, n1_r, j).start()
+        dn1_send[j] = mm(dqkv[r, :], wqkv[...]).astype(BF16)
+        sum_steps(i, BACK, *dn1_sum)
 
         if j == 1:
             c3a = stage3(0, c2a)
             c3b = stage3(1, c2b)
 
-    gl[2, :, 0:576] = mm_tn(n1[...], dqkv[...]).astype(BF16)
-    dmat = dmid[...].reshape(NT * ROWS, 768)
-    gl[2, :, 576:768] = mm_tn(dmat, ofull[t]).astype(BF16)
+    gl[2, 0:576, :] = mm_tn(dqkv[...], n1[...]).astype(BF16)
+    gl[2, 576:768, :] = mm_tn(ofull[t], dmid[...].reshape(NT * ROWS, 768)).astype(BF16)
     c1c = stage1(2)
+    sum_steps(4, BACK, *dn1_sum)
     dsum = jnp.sum(dqkv[...].astype(F32), axis=0, keepdims=True)
     vsend[7:8, :] = jnp.concatenate([dsum, jnp.zeros((1, 192), F32)], axis=1)
     c4a = stage4(0, c3a)
     c4b = stage4(1, c3b)
     c2c = stage2(2, c1c)
-    bo = gathered(bo_send, bo_recv, b_s, b_r)
-    bo_out[...] = mid[own_rows, :] + bo + bproj[...]
-    dn1 = gathered(dn1_send, dn1_recv, n1_s, n1_r)
+    sum_steps(5, BACK, *dn1_sum)
+    sum_steps(4, ORDER, *bo_sum)
+    sum_steps(5, ORDER, *bo_sum)
+    bo = gathered(*bo_sum)
+    bo_out[...] = mid[own_rows, :] + bo + bproj[...][None]
+    dn1 = gathered(*dn1_sum)
     xhat, rstd = norm_stats(x_ref[...].astype(F32))
-    din_out[...] = dmid_own[...] + norm_back(dn1, xhat, rstd, ln1[0:1, :])
+    din_out[...] = dmid_own[...] + norm_back(dn1, xhat, rstd, ln1[0])
     vsend[0:1, :] = jnp.sum(dn1 * xhat, axis=0, keepdims=True)
     vsend[1:2, :] = jnp.sum(dn1, axis=0, keepdims=True)
     cva = [go(vsend, vbuf.at[t], va_s.at[o], va_r.at[o], at_t(o)) for o in range(1, NT)]
@@ -527,20 +614,25 @@
     total = wbuf[0]
     for s in range(1, 8):
         total = total + wbuf[s]
-    vec_out[...] = total * 0.125
+    total = total * 0.125
+    vec_out[...] = total
+    qv_out[0:1, :] = total[7:8, 0:192]
+    qv_out[1:2, :] = total[7:8, 384:576]
     c4a.wait_recv()
     c4b.wait_recv()
     c4c.wait_recv()
 
     for c in pending:
         c.wait_send()
+    for args in ((xfull, x_s, x_r), (gfull, g_s, g_r), (dmid, m_s, m_r)):
+        hop_sent(*args)
     for j in range(NT):
+        hop_sent(ofull, o_s.at[j], o_r.at[j], slice(j * ROWS, (j + 1) * ROWS))
 
         @pl.when(t != j)
         def _():
-            send_block(dn2_send, dn2_recv, n2_s, n2_r, j).wait_send()
-            send_block(bo_send, bo_recv, b_s, b_r, j).wait_send()
-            send_block(dn1_send, dn1_recv, n1_s, n1_r, j).wait_send()
+            for send, recv, ss, rsem in (dn2_sum, bo_sum, dn1_sum):
+                rcopy(send.at[j], recv.at[0, j], ss.at[j], rsem.at[0, j], at_t(1)).wait_send()
 
 
 def on_device_fused(
@@ -548,42 +640,43 @@
     out_bias, second_norm_gain, second_norm_bias, fc_weight, fc_bias, proj_weight, proj_bias,
     out_grad,
 ):
-    wqkv = qkv_weight.reshape(768, 576)
-    bqkv = jnp.concatenate([qv_bias[0], jnp.zeros_like(qv_bias[0]), qv_bias[1]])[None]
-    ln1 = jnp.stack([first_norm_gain, first_norm_bias])
-    ln2 = jnp.stack([second_norm_gain, second_norm_bias, out_bias])
+    wqkv = jnp.transpose(qkv_weight, (1, 2, 0)).reshape(576, 768)
     full = lambda dt: pltpu.VMEM((NT, ROWS, 768), dt)
     head = lambda dt: pltpu.VMEM((3, 512, HD), dt)
     tall = lambda n, dt: pltpu.VMEM((512, n), dt)
     dma = lambda *s: pltpu.SemaphoreType.DMA(s)
+    pair = pltpu.VMEM((2, NT, ROWS, 768), BF16)
+    hops = (2, NT - 1)
     scratch = [
         full(BF16), full(BF16), pltpu.VMEM((NT, NC, 48, 768), BF16), tall(768, BF16),
         head(BF16), head(BF16), head(BF16), pltpu.VMEM((3, 512, 512), F32),
         pltpu.VMEM((NT, 512, 192), BF16), tall(768, F32), tall(768, BF16), tall(768, BF16),
         tall(768, BF16),
-        full(BF16), full(BF16), full(BF16), full(BF16), full(BF16), full(BF16), full(BF16),
+        full(BF16), full(BF16), full(BF16), pair, pair, pair, full(BF16),
         pltpu.VMEM((ROWS, 768), F32),
         head(F32), head(F32), tall(576, BF16),
         pltpu.VMEM((3, 768, 768), BF16), pltpu.VMEM((3, 384, 768), BF16),
         pltpu.VMEM((3, 384, 768), BF16), pltpu.VMEM((3, NC, 96, 768), BF16),
         pltpu.VMEM((8, 768), F32), pltpu.VMEM((NT, 8, 768), F32),
         pltpu.VMEM((8, 768), F32), pltpu.VMEM((8, 8, 768), F32),
-        dma(4), dma(4), dma(4), dma(4), dma(4), dma(4), dma(8), dma(8), pltpu.SemaphoreType.DMA,
-        dma(4, 4), dma(4, 4), dma(4), dma(4), dma(4), dma(4), dma(4), dma(4), dma(4), dma(4),
+        dma(*hops), dma(*hops), dma(*hops), dma(*hops), dma(4), dma(4), dma(8), dma(8), pltpu.SemaphoreType.DMA,
+        dma(4, *hops), dma(4, *hops), dma(4), dma(2, 4), dma(4), dma(2, 4), dma(4), dma(2, 4),
+        dma(*hops), dma(*hops),
         dma(3), dma(3), dma(3, 4), dma(3, 4), dma(3, 4), dma(3, 4), dma(3), dma(3),
         dma(4), dma(4), dma(8), dma(8),
     ]
     vm = pl.BlockSpec(memory_space=pltpu.VMEM)
-    block_out, d_in, grads, vecs = pl.pallas_call(
+    block_out, d_in, grads, vecs, qv = pl.pallas_call(
         layer_kernel,
         out_shape=(
             jax.ShapeDtypeStruct((ROWS, 768), F32),
             jax.ShapeDtypeStruct((ROWS, 768), F32),
             jax.ShapeDtypeStruct((3, 768, 768), BF16),
             jax.ShapeDtypeStruct((8, 768), F32),
+            jax.ShapeDtypeStruct((2, 192), F32),
         ),
-        in_specs=[vm] * 13,
-        out_specs=[vm] * 4,
+        in_specs=[vm] * 15,
+        out_specs=[vm] * 5,
         scratch_shapes=scratch,
         compiler_params=pltpu.CompilerParams(
             collective_id=0, has_side_effects=True, vmem_limit_bytes=60 * 1024 * 1024
@@ -592,8 +685,9 @@
             flops=8_000_000_000, bytes_accessed=12_000_000, transcendentals=2_000_000
         ),
     )(
-        block_in, out_grad, segment_ids.reshape(512, 1), segment_ids, ln1, wqkv, bqkv, out_weight,
-        ln2, fc_weight, fc_bias[None], proj_weight, proj_bias[None],
+        block_in, out_grad, segment_ids, first_norm_gain, first_norm_bias, wqkv, qv_bias,
+        out_weight, out_bias, second_norm_gain, second_norm_bias, fc_weight, fc_bias, proj_weight,
+        proj_bias,
     )
     scaled = lambda a: a.astype(F32) * 0.125
     return (
@@ -601,9 +695,9 @@
         d_in,
         vecs[0],
         vecs[1],
-        scaled(grads[2, :, :576]).reshape(768, 3, 192),
-        jnp.stack([vecs[7, :192], vecs[7, 384:576]]),
-        scaled(grads[2, :, 576:]).T,
+        jnp.transpose(scaled(grads[2, :576]).reshape(3, 192, 768), (2, 0, 1)),
+        qv,
+        scaled(grads[2, 576:]),
         vecs[2],
         vecs[3],
         vecs[4],

time: 187 us -> 147 us (0.79)
  the two profiles are of different devices: /device:TPU:25 before, /device:TPU:17 now
where the time goes in v2:
time: 147 us
  Pallas kernels  135 us (92%)
  other arithmetic  6.85 us (5%)
  local copies, waits for them, and re-layouts  3.76 us (3%)
    pallas_call x1, Pallas kernels, on_device_fused(): pl.pallas_call(layer_kernel, out_shape=(jax.ShapeDtypeStruct((ROWS, 768),...  135 us
    mul x3, other arithmetic, on_device_fused(): scaled = lambda a: a.astype(F32) * 0.125  6.85 us

profile of v2, /device:TPU:17, one launch (start us, length us, event | category | flops | bytes accessed | tf_op | source)
XLA Modules:
  0.0 146.7 jit_solution(11689459764589741876)
XLA Ops:
  0.7 135.4 %shard_map.254 = (f32[128,768]{1,0:T(8,128)}, f32[128,768]{1,0:T(8,128)}, bf16[3,768,768]{2,1,0:T(8,128)(2,1)}, f32[8,768]{1,0:T(8,128)}, f32[2,192]{1,0:T(2,128)}) custom-call(bf16[128,768]{1,0:T(8,128)(2,1)} %x_ref.1, bf16[128,768]{1,0:T(8,128)(2,1)} %g_ref.1, s32[1,512]{1,0:T(1,128)} %seg_row.1, f32[768]{0:T(1024)} %gain1.1, f32[768]{0:T(1024)} %shift1.1, ...), custom_call_target="tpu_custom_call" | custom-call | flops 8000000000 | bytes 12000000 | tf_op jit(solution)/shard_map/pallas_call | solution.py:669
  136.0 0.0 copy-start
  136.0 1.7 %slice_reduce_fusion = (f32[768]{0:T(1024)}, f32[768]{0:T(1024)}, f32[768]{0:T(1024)}, f32[768]{0:T(1024)}, f32[768]{0:T(1024)}, /*index=5*/f32[768]{0:T(1024)}, f32[768]{0:T(1024)}) fusion(f32[8,768]{1,0:T(8,128)} %get-tuple-element.21), kind=kLoop, calls=%fused_computation.4 | loop fusion | bytes 43008 | tf_op jit(solution)/shard_map/slice | solution.py:707
  137.7 1.8 %multiply_bitcast_fusion.2 = f32[192,768]{1,0:T(8,128)} fusion(bf16[3,768,768]{2,1,0:T(8,128)(2,1)} %get-tuple-element.22), kind=kLoop, calls=%fused_computation.3 | loop fusion | flops 294912 | bytes 884736 | tf_op jit(solution)/shard_map/mul | solution.py:692
  139.5 2.5 %convert_multiply_fusion = f32[1,576,768]{2,1,0:T(8,128)} fusion(bf16[3,768,768]{2,1,0:T(8,128)(2,1)} %get-tuple-element.22), kind=kLoop, calls=%fused_computation.2 | loop fusion | flops 884736 | bytes 2654208 | tf_op jit(solution)/shard_map/mul | solution.py:692
  142.0 0.0 copy-done
  142.0 0.0 copy-start.2
  142.0 0.0 copy-start.1
  142.0 0.0 copy-start.3
  142.0 2.5 %multiply_bitcast_fusion = (f32[768,768]{1,0:T(8,128)}, f32[768,768]{1,0:T(8,128)}) fusion(bf16[3,768,768]{2,1,0:T(8,128)(2,1)S(1)} %copy-done), kind=kLoop, calls=%fused_computation | loop fusion | flops 2359296 | bytes 7077888 | tf_op jit(solution)/shard_map/mul | solution.py:692
  144.6 0.0 copy-done.2
  144.6 0.7 copy.32
  145.3 0.0 copy-done.1
  145.3 0.7 copy.33
  146.1 0.0 copy-done.3
  146.1 0.6 copy.34
Async XLA Ops:
  136.0 6.0 %copy-start = (bf16[3,768,768]{2,1,0:T(8,128)(2,1)S(1)}, bf16[3,768,768]{2,1,0:T(8,128)(2,1)}, u32[]{:S(2)}) copy-start(bf16[3,768,768]{2,1,0:T(8,128)(2,1)} %get-tuple-element.22) | copy-start | bytes 10616836
  142.0 2.6 %copy-start.2 = (f32[128,768]{1,0:T(8,128)S(1)}, f32[128,768]{1,0:T(8,128)}, u32[]{:S(2)}) copy-start(f32[128,768]{1,0:T(8,128)} %get-tuple-element.47) | copy-start | bytes 1179652
  142.0 3.3 %copy-start.1 = (f32[128,768]{1,0:T(8,128)S(1)}, f32[128,768]{1,0:T(8,128)}, u32[]{:S(2)}) copy-start(f32[128,768]{1,0:T(8,128)} %get-tuple-element.48) | copy-start | bytes 1179652
  142.0 4.1 %copy-start.3 = (f32[2,192]{1,0:T(2,128)S(1)}, f32[2,192]{1,0:T(2,128)}, u32[]{:S(2)}) copy-start(f32[2,192]{1,0:T(2,128)} %get-tuple-element.52) | copy-start | bytes 4612

commit v3 on v2

--- a/solution.py
+++ b/solution.py
@@ -421,8 +421,6 @@
     far = lax.rem(t + 2, NT)
     project(far)
     project(far + 1 - 2 * lax.rem(far, 2))
-    hop_wait(0, gfull, g_s, g_r)
-    hop_send(1, gfull, g_s, g_r)
     cw2 = [go(wpart, wpart, w2_s.at[o], w2_r.at[o], at_d(o)) for o in range(1, 8)]
 
     def o_hops(i):
@@ -450,7 +448,10 @@
             outs.append(mm(p.astype(BF16), vh[h, :n, :]))
         ofull[t, r, :] = jnp.concatenate(outs, axis=1).astype(BF16)
         o_hops(i)
-        if i == 1:
+        if i == 0:
+            hop_wait(0, gfull, g_s, g_r)
+            hop_send(1, gfull, g_s, g_r)
+        if i == 2:
             hop_wait(1, gfull, g_s, g_r)
             hop_send(2, gfull, g_s, g_r)
 
@@ -534,8 +535,6 @@
     dmid_own[...] = dm
     dmid[t] = dm.astype(BF16)
     hop_send(0, dmid, m_s, m_r)
-    sum_steps(0, ORDER, *bo_sum)
-    sum_steps(1, ORDER, *bo_sum)
     vsend[2:3, :] = jnp.sum(dm, axis=0, keepdims=True)
     vsend[3:4, :] = jnp.sum(dn2 * xhat, axis=0, keepdims=True)
     vsend[4:5, :] = jnp.sum(dn2, axis=0, keepdims=True)
@@ -549,9 +548,8 @@
     hop_wait(1, dmid, m_s, m_r)
     hop_send(2, dmid, m_s, m_r)
     c2b = stage2(1, c1b)
-    sum_steps(2, ORDER, *bo_sum)
-    sum_steps(3, ORDER, *bo_sum)
     hop_wait(2, dmid, m_s, m_r)
+    sum_steps(0, ORDER, *bo_sum)
 
     dkacc[...] = jnp.zeros_like(dkacc)
     dvacc[...] = jnp.zeros_like(dvacc)
@@ -575,6 +573,8 @@
         dqkv[r, :] = jnp.concatenate(parts, axis=1).astype(BF16)
         dn1_send[j] = mm(dqkv[r, :], wqkv[...]).astype(BF16)
         sum_steps(i, BACK, *dn1_sum)
+        if i < 3:
+            sum_steps(i + 1, ORDER, *bo_sum)
 
         if j == 1:
             c3a = stage3(0, c2a)

time: 147 us -> 147 us (level); the launches traced: 147 us -> 144 us
  Pallas kernels: 135 us -> 133 us
    pallas_call x1, Pallas kernels: 135 us -> 133 us  [on_device_fused(): pl.pallas_call(layer_kernel, out_shape=(jax.ShapeDtypeStruct((ROWS, 768),...]
where the time goes in v3:
time: 147 us; the launch traced here: 144 us
  Pallas kernels  133 us (90%)
  other arithmetic  6.85 us (5%)
  local copies, waits for them, and re-layouts  3.76 us (3%)
    pallas_call x1, Pallas kernels, on_device_fused(): pl.pallas_call(layer_kernel, out_shape=(jax.ShapeDtypeStruct((ROWS, 768),...  133 us
    mul x3, other arithmetic, on_device_fused(): scaled = lambda a: a.astype(F32) * 0.125  6.85 us

profile of v3, /device:TPU:17, one launch (start us, length us, event | category | flops | bytes accessed | tf_op | source)
XLA Modules:
  0.0 144.5 jit_solution(7569841628649608178)
XLA Ops:
  0.7 133.2 %shard_map.254 = (f32[128,768]{1,0:T(8,128)}, f32[128,768]{1,0:T(8,128)}, bf16[3,768,768]{2,1,0:T(8,128)(2,1)}, f32[8,768]{1,0:T(8,128)}, f32[2,192]{1,0:T(2,128)}) custom-call(bf16[128,768]{1,0:T(8,128)(2,1)} %x_ref.1, bf16[128,768]{1,0:T(8,128)(2,1)} %g_ref.1, s32[1,512]{1,0:T(1,128)} %seg_row.1, f32[768]{0:T(1024)} %gain1.1, f32[768]{0:T(1024)} %shift1.1, ...), custom_call_target="tpu_custom_call" | custom-call | flops 8000000000 | bytes 12000000 | tf_op jit(solution)/shard_map/pallas_call | solution.py:669
  133.9 0.0 copy-start
  133.9 1.7 %slice_reduce_fusion = (f32[768]{0:T(1024)}, f32[768]{0:T(1024)}, f32[768]{0:T(1024)}, f32[768]{0:T(1024)}, f32[768]{0:T(1024)}, /*index=5*/f32[768]{0:T(1024)}, f32[768]{0:T(1024)}) fusion(f32[8,768]{1,0:T(8,128)} %get-tuple-element.21), kind=kLoop, calls=%fused_computation.4 | loop fusion | bytes 43008 | tf_op jit(solution)/shard_map/slice | solution.py:707
  135.5 1.8 %multiply_bitcast_fusion.2 = f32[192,768]{1,0:T(8,128)} fusion(bf16[3,768,768]{2,1,0:T(8,128)(2,1)} %get-tuple-element.22), kind=kLoop, calls=%fused_computation.3 | loop fusion | flops 294912 | bytes 884736 | tf_op jit(solution)/shard_map/mul | solution.py:692
  137.4 2.5 %convert_multiply_fusion = f32[1,576,768]{2,1,0:T(8,128)} fusion(bf16[3,768,768]{2,1,0:T(8,128)(2,1)} %get-tuple-element.22), kind=kLoop, calls=%fused_computation.2 | loop fusion | flops 884736 | bytes 2654208 | tf_op jit(solution)/shard_map/mul | solution.py:692
  139.8 0.0 copy-done
  139.9 0.0 copy-start.2
  139.9 0.0 copy-start.1
  139.9 0.0 copy-start.3
  139.9 2.5 %multiply_bitcast_fusion = (f32[768,768]{1,0:T(8,128)}, f32[768,768]{1,0:T(8,128)}) fusion(bf16[3,768,768]{2,1,0:T(8,128)(2,1)S(1)} %copy-done), kind=kLoop, calls=%fused_computation | loop fusion | flops 2359296 | bytes 7077888 | tf_op jit(solution)/shard_map/mul | solution.py:692
  142.4 0.0 copy-done.2
  142.4 0.7 copy.32
  143.2 0.0 copy-done.1
  143.2 0.7 copy.33
  143.9 0.0 copy-done.3
  143.9 0.6 copy.34
Async XLA Ops:
  133.9 6.0 %copy-start = (bf16[3,768,768]{2,1,0:T(8,128)(2,1)S(1)}, bf16[3,768,768]{2,1,0:T(8,128)(2,1)}, u32[]{:S(2)}) copy-start(bf16[3,768,768]{2,1,0:T(8,128)(2,1)} %get-tuple-element.22) | copy-start | bytes 10616836
  139.9 2.6 %copy-start.2 = (f32[128,768]{1,0:T(8,128)S(1)}, f32[128,768]{1,0:T(8,128)}, u32[]{:S(2)}) copy-start(f32[128,768]{1,0:T(8,128)} %get-tuple-element.47) | copy-start | bytes 1179652
  139.9 3.3 %copy-start.1 = (f32[128,768]{1,0:T(8,128)S(1)}, f32[128,768]{1,0:T(8,128)}, u32[]{:S(2)}) copy-start(f32[128,768]{1,0:T(8,128)} %get-tuple-element.48) | copy-start | bytes 1179652
  139.9 4.1 %copy-start.3 = (f32[2,192]{1,0:T(2,128)S(1)}, f32[2,192]{1,0:T(2,128)}, u32[]{:S(2)}) copy-start(f32[2,192]{1,0:T(2,128)} %get-tuple-element.52) | copy-start | bytes 4612
